TPU v7x, 32 devices: a whole 2x2x4 slice. The times are simulated.
32 devices in a mesh: user: 16 (over z, y, core), item: 2 (over x).
Axes of the slice: x: 2, y: 2, z: 4, core: 2. Of those that a mesh axis runs over, the one named last changes fastest.
Arguments:
- observed: bfloat16 [32, 128, 128, 128], P(('user', 'item')), may hold values from -6 to 6
- user_block: int32 [32], P(('user', 'item')), may hold values from 0 to 3
- item_block: int32 [32], P(('user', 'item')), may hold values from 0 to 1
- stratum: int32 [32], P(('user', 'item')), may hold values from 0 to 1
- context_ids: int32 [32, 128], P(('user', 'item')), may hold values from 0 to 255
- core_tensor: float32 [16384, 128], P(('user', 'item')), may hold values from -1 to 1
- user_factor: bfloat16 [8192, 128], P('user'), may hold values from -3 to 3
- item_factor: bfloat16 [512, 128], P('item'), may hold values from -3 to 3
- context_factor: bfloat16 [256, 128], P(('user', 'item')), may hold values from -3 to 3
Outputs:
- core_grad: float32 [16384, 128], P(('user', 'item'))
- user_grad: float32 [8192, 128], P(('user', 'item'))
- item_grad: float32 [512, 128], P(('user', 'item'))
- context_grad: float32 [256, 128], P(('user', 'item'))
Inputs may be any that keep to these rules, and one draw needn't show every extreme that they name: `user_block`: user block within the tile's user index.
All inputs are finite; a program needn't handle non-finite values.
Results may differ from a plain program's by a relative error of at most 0.0031.
Values may be sent and summed in bfloat16 or wider, within the bound.
A program may use at most 128 MiB of HBM per device.

v0:
```python
import math

import jax
import jax.numpy as jnp
from jax import lax
from jax.sharding import PartitionSpec as P


def contract_last(left, right):
    return lax.dot_general(
        left, right, (((1,), (1,)), ((), ())), preferred_element_type=jnp.float32
    )


def contract_first(left, right):
    return lax.dot_general(
        left, right, (((0,), (0,)), ((), ())), preferred_element_type=jnp.float32
    )


def tile_terms(core_half, user_rows, item_rows, ctx_rows, observed_tile):
    rank_one = user_rows.shape[1]
    rank_two = item_rows.shape[1]
    block_user, block_item, slices = observed_tile.shape
    first_pass = contract_last(core_half, ctx_rows).astype(jnp.bfloat16)
    first_cube = first_pass.reshape(rank_one, rank_two, slices)
    second = jnp.einsum(
        "pqc,bq->pbc", first_cube, item_rows, preferred_element_type=jnp.float32
    ).astype(jnp.bfloat16)
    second_flat = second.reshape(rank_one, block_item * slices)
    predicted = jnp.dot(user_rows, second_flat, preferred_element_type=jnp.float32)
    residual = (
        predicted - observed_tile.reshape(block_user, block_item * slices).astype(jnp.float32)
    ).astype(jnp.bfloat16)
    grad_user = contract_last(residual, second_flat)
    back_flat = contract_first(user_rows, residual).astype(jnp.bfloat16)
    back_cube = back_flat.reshape(rank_one, block_item, slices)
    grad_item = jnp.einsum("pbc,pqc->bq", back_cube, first_cube, preferred_element_type=jnp.float32)
    folded = jnp.einsum(
        "pbc,bq->pqc", back_cube, item_rows, preferred_element_type=jnp.float32
    ).astype(jnp.bfloat16)
    folded = folded.reshape(rank_one * rank_two, slices)
    grad_ctx = contract_first(folded, core_half)
    grad_core = jnp.dot(folded, ctx_rows, preferred_element_type=jnp.float32)
    return (grad_core, grad_user, grad_item, grad_ctx)


def local(
    observed,
    user_block,
    item_block,
    stratum,
    context_ids,
    core_tensor,
    user_factor,
    item_factor,
    context_factor,
):
    core_half = core_tensor.astype(jnp.bfloat16)
    item_all = lax.all_gather(item_factor, "item", axis=0, tiled=True)
    core_all, context_all = (
        lax.all_gather(core_half, ("user", "item"), axis=0, tiled=True),
        lax.all_gather(context_factor, ("user", "item"), axis=0, tiled=True),
    )
    tiles_here, block_user, block_item, slices = observed.shape
    blocks_stratum = item_factor.shape[0] // block_item
    count_ctx = context_all.shape[0]
    scale = 1.0 / math.sqrt(block_user * block_item * slices)
    columns = jnp.arange(count_ctx, dtype=jnp.int32)

    def one_tile(index, carry):
        acc_core, acc_user, acc_item, acc_ctx = carry
        user_start = user_block[index] * block_user
        item_start = (stratum[index] * blocks_stratum + item_block[index]) * block_item
        user_rows = lax.dynamic_slice_in_dim(user_factor, user_start, block_user, 0)
        item_rows = lax.dynamic_slice_in_dim(item_all, item_start, block_item, 0)
        slice_ids = context_ids[index]
        ctx_rows = jnp.take(context_all, slice_ids, axis=0)
        g_core, g_user, g_item, g_ctx = tile_terms(
            core_all, user_rows, item_rows, ctx_rows, observed[index]
        )
        old_user = lax.dynamic_slice_in_dim(acc_user, user_start, block_user, 0)
        acc_user = lax.dynamic_update_slice_in_dim(acc_user, old_user + g_user, user_start, 0)
        old_item = lax.dynamic_slice_in_dim(acc_item, item_start, block_item, 0)
        acc_item = lax.dynamic_update_slice_in_dim(acc_item, old_item + g_item, item_start, 0)
        picker = (slice_ids[:, None] == columns[None, :]).astype(jnp.float32)
        acc_ctx = acc_ctx + lax.dot_general(
            picker,
            g_ctx,
            (((0,), (0,)), ((), ())),
            precision=lax.Precision.HIGHEST,
            preferred_element_type=jnp.float32,
        )
        return (acc_core + g_core, acc_user, acc_item, acc_ctx)

    init = (
        jnp.zeros(core_all.shape, jnp.float32),
        jnp.zeros(user_factor.shape, jnp.float32),
        jnp.zeros(item_all.shape, jnp.float32),
        jnp.zeros(context_all.shape, jnp.float32),
    )
    acc_core, acc_user, acc_item, acc_ctx = lax.fori_loop(0, tiles_here, one_tile, init)
    term_core = acc_core * scale
    term_user = acc_user * scale
    term_item = acc_item * scale
    term_ctx = acc_ctx * scale
    core_mid, item_mid, ctx_mid = (
        lax.psum_scatter(term_core, "user", scatter_dimension=0, tiled=True),
        lax.psum_scatter(term_item, "user", scatter_dimension=0, tiled=True),
        lax.psum_scatter(term_ctx, "user", scatter_dimension=0, tiled=True),
    )
    core_grad, item_grad, context_grad, user_grad = (
        lax.psum_scatter(core_mid, "item", scatter_dimension=0, tiled=True),
        lax.psum_scatter(item_mid, "item", scatter_dimension=0, tiled=True),
        lax.psum_scatter(ctx_mid, "item", scatter_dimension=0, tiled=True),
        lax.psum_scatter(term_user, "item", scatter_dimension=0, tiled=True),
    )
    return (core_grad, user_grad, item_grad, context_grad)


def solution(mesh):
    return jax.shard_map(
        local,
        mesh=mesh,
        in_specs=(
            P(("user", "item"), None, None, None),
            P(("user", "item")),
            P(("user", "item")),
            P(("user", "item")),
            P(("user", "item"), None),
            P(("user", "item"), None),
            P("user", None),
            P("item", None),
            P(("user", "item"), None),
        ),
        out_specs=(
            P(("user", "item"), None),
            P(("user", "item"), None),
            P(("user", "item"), None),
            P(("user", "item"), None),
        ),
        check_vma=False,
    )
```

profile of v0, /device:TPU:0, one launch (start us, length us, event | category | flops | bytes accessed | tf_op | source)
XLA Modules:
  0.0 393.5 jit_solution(11647900617548232596)
XLA Ops:
  7.2 1.6 convert_element_type.41
  8.9 0.0 reduce-scatter.13.cloned.1.call-start
  10.9 6.5 %convert.2 = f32[16,8,128,128]{3,2,1,0:T(8,128)} convert(bf16[16,8,128,128]{3,2,1,0:T(8,128)(2,1)} %bitcast.70) | non-fusion elementwise | flops 2097152 | bytes 12582912
  17.4 70.4 %all_gather.10 = bf16[256,128]{1,0:T(8,128)(2,1)S(1)} all-gather(bf16[8,128]{1,0:T(8,128)(2,1)S(1)} %copy-done.4), channel_id=1, replica_groups=mesh['user'=16,'item'=2] {'user','item'}, dimensions={0}, use_global_device_ids=true | all-gather | bytes 67584 | tf_op jit(solution)/shard_map/all_gather | solution.py:63
  87.8 0.7 gather_fusion
  88.5 4.9 %all_gather.9 = bf16[512,128]{1,0:T(8,128)(2,1)S(1)} all-gather(bf16[256,128]{1,0:T(8,128)(2,1)S(1)} %copy-done.3), channel_id=1, replica_groups=mesh['user'=16,'item'=2] {'item'}, dimensions={0}, use_global_device_ids=true | all-gather | bytes 196608 | tf_op jit(solution)/shard_map/all_gather | solution.py:60
  93.5 3.6 fusion.15
  97.2 1.3 fusion.12
  98.5 0.9 slice-done.1
  99.4 18.2 %fusion = bf16[128,16384]{1,0:T(8,128)(2,1)S(1)} fusion(f32[16,8,128,128]{3,2,1,0:T(8,128)S(1)} %bitcast.65, bf16[16,8,128,128]{3,2,1,0:T(8,128)(2,1)S(1)} %bitcast.66, bf16[512,128]{1,0:T(8,128)(2,1)S(1)} %copy-done, s32[]{:T(128)S(6)} %select_n.41), kind=kOutput, calls=%fused_computation.3 | convolution fusion | flops 541065216 | bytes 16809988 | tf_op jit(solution)/shard_map/while/body/eval_jaxpr/dot_general | solution.py:31
  117.6 1.3 fusion.16
  118.9 0.6 copy-done.2
  119.5 1.2 copy.26
  120.8 3.3 convolution_convert_fusion.2
  124.1 1.4 fusion.23
  125.4 0.7 broadcast_multiply_fusion
  126.2 0.0 reduce-scatter.7.cloned.1.call-start
  126.2 6.7 %convolution_multiply_fusion = f32[16384,128]{1,0:T(8,128)} fusion(bf16[16384,128]{1,0:T(8,128)(2,1)} %bitcast.62, bf16[128,128]{1,0:T(8,128)(2,1)S(1)} %gather_fusion, pred[128]{0:T(512)(128)(4,1)S(1)} %compare_and_fusion), kind=kOutput, calls=%fused_computation.1 | convolution fusion | flops 538984448 | bytes 12615808 | tf_op jit(solution)/shard_map/while/body/eval_jaxpr/dot_general | solution.py:44
  133.0 4.8 %fusion.40 = f32[128,128]{1,0:T(8,128)S(1)} fusion(bf16[16384,128]{1,0:T(8,128)(2,1)} %bitcast.63, bf16[16384,128]{1,0:T(8,128)(2,1)} %all-gather.2.cloned.1.call-done), kind=kOutput, calls=%fused_computation.48 | convolution fusion | flops 536870912 | bytes 8454144 | tf_op jit(solution)/shard_map/while/body/eval_jaxpr/dot_general | solution.py:16
  137.8 1.0 convolution_multiply_fusion.1
  138.9 0.0 reduce-scatter.15.cloned.1.call-start
  139.0 7.9 %fusion.17 = f32[512,128]{1,0:T(8,128)S(1)} fusion(f32[512,128]{1,0:T(8,128)S(1)} %broadcast.32.clone, s32[]{:T(128)S(6)} %select_n.41, bf16[128,16384]{1,0:T(8,128)(2,1)} %copy-done.2, bf16[16,8,128,128]{3,2,1,0:T(8,128)(2,1)} %bitcast.67), kind=kOutput, calls=%fused_computation.22 | convolution fusion | flops 536870912 | bytes 8454148 | tf_op jit(solution)/shard_map/while/body/eval_jaxpr/dot_general | solution.py:10
  146.9 30.6 %reduce-scatter.13.cloned.1.call-done = f32[32,128]{1,0:T(8,128)} async-done(((f32[512,128]{1,0:T(8,128)}), f32[32,128]{1,0:T(8,128)}) %reduce-scatter.13.cloned.1.call-update) | async-done | bytes 16400 | tf_op jit(solution)/shard_map/reduce_scatter | solution.py:109
  177.6 0.7 broadcast_multiply_fusion.1
  178.4 106.9 %reduce-scatter.7.cloned.1.call-done = f32[1024,128]{1,0:T(8,128)} async-done(((f32[16384,128]{1,0:T(8,128)}), f32[1024,128]{1,0:T(8,128)}) %reduce-scatter.7.cloned.1.call-update) | async-done | bytes 524304 | tf_op jit(solution)/shard_map/reduce_scatter | solution.py:108
  285.3 0.6 dynamic-slice
  286.5 56.8 %reduce-scatter.17.cloned.1.call-done = f32[16,128]{1,0:T(8,128)} async-done(((f32[256,128]{1,0:T(8,128)}), f32[16,128]{1,0:T(8,128)}) %reduce-scatter.17.cloned.1.call-update) | async-done | bytes 8208 | tf_op jit(solution)/shard_map/reduce_scatter | solution.py:110
  343.4 5.1 %all-reduce = f32[16,128]{1,0:T(8,128)S(1)} all-reduce(f32[16,128]{1,0:T(8,128)} %reduce-scatter.17.cloned.1.call-done), channel_id=8, replica_groups=mesh['user'=16,'item'=2] {'item'}, use_global_device_ids=true, to_apply=%region_6.7.clone | all-reduce | flops 2048 | bytes 16384
  348.5 0.6 constant_dynamic-slice_fusion
  349.1 5.7 %reduce-scatter.15.cloned.1.call-done = f32[16,128]{1,0:T(8,128)} async-done(((f32[32,128]{1,0:T(8,128)}), f32[16,128]{1,0:T(8,128)}) %reduce-scatter.15.cloned.1.call-update) | async-done | bytes 8208 | tf_op jit(solution)/shard_map/reduce_scatter | solution.py:114
  354.8 14.3 %reduce-scatter.11.cloned.1.call-done = f32[256,128]{1,0:T(8,128)} async-done(((f32[512,128]{1,0:T(8,128)}), f32[256,128]{1,0:T(8,128)}) %reduce-scatter.11.cloned.1.call-update) | async-done | bytes 131088 | tf_op jit(solution)/shard_map/reduce_scatter | solution.py:116
  369.1 17.5 %reduce-scatter.9.cloned.1.call-done = f32[512,128]{1,0:T(8,128)} async-done(((f32[1024,128]{1,0:T(8,128)}), f32[512,128]{1,0:T(8,128)}) %reduce-scatter.9.cloned.1.call-update) | async-done | bytes 262160 | tf_op jit(solution)/shard_map/reduce_scatter | solution.py:113
  (34 shorter events, 0.4 us)
Async XLA Ops:
  7.2 91.3 %copy-start = (bf16[512,128]{1,0:T(8,128)(2,1)S(1)}, bf16[512,128]{1,0:T(8,128)(2,1)}, u32[]{:S(2)}) copy-start(bf16[512,128]{1,0:T(8,128)(2,1)} %param.15) | copy-start | bytes 393220
  7.2 86.3 %all-gather.2.cloned.1.call-start = ((), (), s32[]{:S(2)}) async-start(), calls=%async_computation.6 | async-start | bytes 4325376 | tf_op jit(solution)/shard_map/all_gather | solution.py:62
  8.9 168.6 %reduce-scatter.13.cloned.1.call-start = ((), (), s32[]{:S(2)}) async-start(), calls=%async_computation.10 | async-start | bytes 278528 | tf_op jit(solution)/shard_map/reduce_scatter | solution.py:109
  10.9 6.5 %copy-start.4 = (bf16[8,128]{1,0:T(8,128)(2,1)S(1)}, bf16[8,128]{1,0:T(8,128)(2,1)}, u32[]{:S(2)}) copy-start(bf16[8,128]{1,0:T(8,128)(2,1)} %param.17) | copy-start | bytes 6148
  10.9 76.9 %copy-start.5 = (s32[1,128]{1,0:T(1,128)S(1)}, s32[1,128]{1,0:T(1,128)}, u32[]{:S(2)}) copy-start(s32[1,128]{1,0:T(1,128)} %param.13) | copy-start | bytes 1540
  10.9 77.6 %copy-start.3 = (bf16[256,128]{1,0:T(8,128)(2,1)S(1)}, bf16[256,128]{1,0:T(8,128)(2,1)}, u32[]{:S(2)}) copy-start(bf16[256,128]{1,0:T(8,128)(2,1)} %param.16) | copy-start | bytes 196612
  93.5 4.9 %slice-start = ((s8[8388608]{0:T(1024)(128)(4,1)}), s8[4194304]{0:T(1024)(128)(4,1)S(1)}, s32[]{:S(2)}) async-start(s8[8388608]{0:T(1024)(128)(4,1)} %bitcast.64), calls=%async_computation.13 | async-start | bytes 8388608
  97.2 2.2 slice-start.1
  98.4 19.2 %copy-start.1 = (bf16[128,128,128]{2,0,1:T(8,128)(2,1)}, bf16[128,128,128]{2,0,1:T(8,128)(2,1)S(1)}, u32[]{:S(2)}) copy-start(bf16[128,128,128]{2,0,1:T(8,128)(2,1)S(1)} %fusion.12) | copy-start | bytes 12582916
  117.6 1.9 copy-start.2
  126.2 159.1 %reduce-scatter.7.cloned.1.call-start = ((), (), s32[]{:S(2)}) async-start(), calls=%async_computation.7 | async-start | bytes 8912896 | tf_op jit(solution)/shard_map/reduce_scatter | solution.py:108
  133.0 210.4 %reduce-scatter.17.cloned.1.call-start = ((), (), s32[]{:S(2)}) async-start(), calls=%async_computation.12 | async-start | bytes 139264 | tf_op jit(solution)/shard_map/reduce_scatter | solution.py:110
  138.9 215.9 %reduce-scatter.15.cloned.1.call-start = ((), (), s32[]{:S(2)}) async-start(), calls=%async_computation.11 | async-start | bytes 24576 | tf_op jit(solution)/shard_map/reduce_scatter | solution.py:114
  138.9 146.3 %copy-start.6 = (u32[32]{0:T(128)S(1)}, u32[32]{0:T(128)}, u32[]{:S(2)}) copy-start(u32[32]{0:T(128)} %constant.55) | copy-start | bytes 388
  177.5 191.6 %reduce-scatter.11.cloned.1.call-start = ((), (), s32[]{:S(2)}) async-start(), calls=%async_computation.9 | async-start | bytes 393216 | tf_op jit(solution)/shard_map/reduce_scatter | solution.py:116
  178.3 208.3 %reduce-scatter.9.cloned.1.call-start = ((), (), s32[]{:S(2)}) async-start(), calls=%async_computation.8 | async-start | bytes 786432 | tf_op jit(solution)/shard_map/reduce_scatter | solution.py:113
Sparse Core Ops, SparseCore 0:
  11.6 65.1 all-gather.1
  126.3 51.1 reduce-scatter.12
  181.6 103.6 reduce-scatter.6
  288.6 54.7 reduce-scatter.16
  346.0 8.7 reduce-scatter.14
  357.5 11.6 reduce-scatter.10
  372.1 14.5 reduce-scatter.8
where the time goes:
time: 394 us; the launch traced here: 393 us
  waiting for transfers between devices  232 us (59%)
  blocking collectives  80.4 us (20%)
  matrix products  49.5 us (13%)
  between operations  16.9 us (4%)
  other arithmetic  9.65 us (2%)
  local copies, waits for them, and re-layouts  4.72 us (1%)
    reduce_scatter x1, waiting for transfers between devices, local(): lax.psum_scatter(term_core, 'user', scatter_dimension=0, tiled=True)  107 us
    all_gather x1, blocking collectives, local(): lax.all_gather(context_factor, ('user', 'item'), axis=0, tiled=True)  70.4 us
    reduce_scatter x1, waiting for transfers between devices, local(): lax.psum_scatter(term_ctx, 'user', scatter_dimension=0, tiled=True)  56.8 us
    reduce_scatter x1, waiting for transfers between devices, local(): lax.psum_scatter(term_item, 'user', scatter_dimension=0, tiled=True)  30.6 us
    dot_general x1, matrix products, tile_terms(): jnp.dot(user_rows, second_flat, preferred_element_type=jnp.float32)  18.2 us
    reduce_scatter x1, waiting for transfers between devices, local(): lax.psum_scatter(core_mid, 'item', scatter_dimension=0, tiled=True)  17.5 us
    reduce_scatter x1, waiting for transfers between devices, local(): lax.psum_scatter(term_user, 'item', scatter_dimension=0, tiled=True)  14.3 us
    dot_general x2, matrix products, contract_last(): lax.dot_general(left, right, (((1,), (1,)), ((), ())), preferred_element_...  11.6 us
  transfers between devices with their start and end apart: 7, of which 6 were waited for; matrix products, arithmetic and copies ran while one was open for 8% of the time, Pallas kernels for 0%

commit v1 on v0

v1 whole, which is shorter than its diff:
```python
import functools
import math

import jax
import jax.numpy as jnp
from jax import lax
from jax.experimental import pallas as pl
from jax.experimental.pallas import tpu as pltpu
from jax.sharding import PartitionSpec as P

MESH = pl.DeviceIdType.MESH
F32 = jnp.float32
BF16 = jnp.bfloat16
VMEM_LIMIT = 56 * 1024 * 1024


def up16(rows):
    return (rows + 15) // 16 * 16


def dot(left, right, left_dim, right_dim):
    return lax.dot_general(
        left, right, (((left_dim,), (right_dim,)), ((), ())), preferred_element_type=F32
    )


class Grid:
    def __init__(self, users, items):
        nc = 2 if users % 2 == 0 else 1
        rest = users // nc
        ny = 1
        while rest % (2 * ny) == 0 and (2 * ny) * (2 * ny) <= rest:
            ny *= 2
        self.n = {"z": rest // ny, "y": ny, "c": nc, "x": items}

    def here(self):
        user = lax.axis_index("user")
        n = self.n
        return {
            "c": lax.rem(user, n["c"]),
            "y": lax.rem(lax.div(user, n["c"]), n["y"]),
            "z": lax.div(user, n["c"] * n["y"]),
            "x": lax.axis_index("item"),
        }

    def moved(self, at, **steps):
        out = dict(at)
        for axis, step in steps.items():
            if step:
                out[axis] = lax.rem(at[axis] + step + self.n[axis], self.n[axis])
        return out

    def device(self, at):
        n = self.n
        return ((at["z"] * n["y"] + at["y"]) * n["c"] + at["c"], at["x"])

    def shard(self, at):
        user, item = self.device(at)
        return user * self.n["x"] + item

    def partners(self, at):
        return [
            self.moved(at, **{axis: step})
            for axis in "zycx"
            for step in range(1, self.n[axis])
        ]


def enter(grid, at):
    barrier = pltpu.get_barrier_semaphore()
    others = grid.partners(at)
    for other in others:
        pl.semaphore_signal(barrier, inc=1, device_id=grid.device(other), device_id_type=MESH)
    pl.semaphore_wait(barrier, len(others))


class Wires:
    def __init__(self, grid, send_sems, recv_sems):
        self.grid, self.send, self.recv, self.used, self.copies = grid, send_sems, recv_sems, 0, []

    def start(self, src, dst, to):
        copy = pltpu.make_async_remote_copy(
            src_ref=src,
            dst_ref=dst,
            send_sem=self.send.at[self.used],
            recv_sem=self.recv.at[self.used],
            device_id=self.grid.device(to),
            device_id_type=MESH,
        )
        copy.start()
        self.used += 1
        self.copies.append(copy)
        return copy

    def finish(self):
        for copy in self.copies:
            copy.wait_send()


def halves(rows):
    first = up16(rows // 2)
    return (0, first), (first, rows - first)


def order(n):
    return [(step + 1) % n for step in range(n)]


def gather_kernel(grid, shard_ref, out_ref, send_sems, recv_sems):
    n = grid.n
    at = grid.here()
    rows = shard_ref.shape[0]
    out_ref[grid.shard(at)] = shard_ref[...]
    enter(grid, at)
    wires = Wires(grid, send_sems, recv_sems)

    def send(owner, part, **to):
        ref = out_ref.at[grid.shard(owner), pl.ds(*part)]
        return wires.start(ref, ref, grid.moved(at, **to))

    parts = [(part, *axes) for part, axes in zip(halves(rows), (("y", "x"), ("x", "y")))]
    first = {}
    for dz in range(1, n["z"]):
        for part, one, two in parts:
            first[dz, part] = send(at, part, z=dz)
    pending = []
    for dz in range(n["z"]):
        second = {}
        for part, one, two in parts:
            if dz:
                first[dz, part].wait_recv()
            mine = grid.moved(at, z=-dz)
            for d1 in range(1, n[one]):
                second[d1, part] = send(mine, part, **{one: d1})
        third = {}
        for part, one, two in parts:
            for d1 in range(n[one]):
                if d1:
                    second[d1, part].wait_recv()
                mine = grid.moved(at, **{"z": -dz, one: -d1})
                for d2 in range(1, n[two]):
                    third[d1, d2, part] = send(mine, part, **{two: d2})
        for part, one, two in parts:
            for d1 in range(n[one]):
                for d2 in range(n[two]):
                    if d2:
                        third[d1, d2, part].wait_recv()
                    mine = grid.moved(at, **{"z": -dz, one: -d1, two: -d2})
                    for dc in range(1, n["c"]):
                        pending.append(send(mine, part, c=dc))
    for copy in pending:
        copy.wait_recv()
    wires.finish()


def gather(grid, shard):
    n = grid.n
    total = n["z"] * n["y"] * n["c"] * n["x"]
    copies = 2 * (total - 1)
    return pl.pallas_call(
        functools.partial(gather_kernel, grid),
        out_shape=jax.ShapeDtypeStruct((total,) + shard.shape, shard.dtype),
        in_specs=[pl.BlockSpec(memory_space=pltpu.VMEM)],
        out_specs=pl.BlockSpec(memory_space=pltpu.VMEM),
        scratch_shapes=[pltpu.SemaphoreType.DMA((copies,)), pltpu.SemaphoreType.DMA((copies,))],
        compiler_params=pltpu.CompilerParams(
            collective_id=0, has_side_effects=True, vmem_limit_bytes=VMEM_LIMIT
        ),
        name="gather_factors",
    )(shard)


def tile_kernel(
    sizes, index_ref, ids_ref, observed_ref, all_ref, user_ref, terms_ref, user_out_ref,
    observed32_ref, first_ref, cube_ref,
):
    m, ni, nk, items, blocks, scale = sizes
    total, rows, _ = all_ref.shape
    bu, bi, kc = observed_ref.shape
    rank_two = kc_rank = all_ref.shape[2]
    rank_one = total * m // rank_two
    item_at, ctx_at = m, m + up16(ni)
    ctx_pad = rows - ctx_at
    user_block, item_block, stratum = index_ref[0], index_ref[1], index_ref[2]
    unit = max(m, 4 * rank_two)
    per, across = unit // m, unit // rank_two

    user_start = pl.multiple_of(user_block * bu, bu)
    user_rows = user_ref[pl.ds(user_start, bu), :]
    item_first = (item_block * (bi // ni)) * items + stratum
    item_rows = jnp.concatenate(
        [
            all_ref[item_first + j * items, pl.ds(item_at, up16(ni)), :].astype(F32)[:ni]
            for j in range(bi // ni)
        ],
        axis=0,
    ).astype(BF16)
    ids = ids_ref[...]
    places = lax.div(ids, jnp.full_like(ids, nk)) * ctx_pad + lax.rem(ids, jnp.full_like(ids, nk))
    spots = lax.broadcasted_iota(jnp.int32, (total * ctx_pad, kc), 0)
    picker = jnp.where(spots == places, 1.0, 0.0).astype(BF16)
    ctx_all = all_ref[:, pl.ds(ctx_at, ctx_pad), :].reshape(total * ctx_pad, kc_rank)
    ctx_rows = dot(picker, ctx_all, 0, 0).astype(BF16)

    def widen(a, carry):
        start = pl.multiple_of(a * bi, bi)
        observed32_ref[pl.ds(start, bi), :] = observed_ref[a].astype(F32)
        return carry

    lax.fori_loop(0, bu, widen, 0, unroll=4)

    def core_of(k):
        pieces = [all_ref[k * per + j, pl.ds(0, m), :] for j in range(per)]
        return pieces[0] if per == 1 else jnp.concatenate(pieces, axis=0)

    def forward(k, carry):
        first = dot(core_of(k), ctx_rows, 1, 1).astype(BF16)
        first_ref[pl.ds(pl.multiple_of(k * unit, unit), unit), :] = first
        wide = jnp.concatenate(
            [first[j * rank_two:(j + 1) * rank_two] for j in range(across)], axis=1
        )
        second = dot(item_rows, wide, 1, 0)
        for j in range(across):
            start = pl.multiple_of((k * across + j) * bi, bi)
            cube_ref[pl.ds(start, bi), :] = second[:, j * kc:(j + 1) * kc]
        return carry

    lax.fori_loop(0, total * m // unit, forward, 0)

    wide_b = 4

    def middle(k, grad_user):
        b = k * wide_b
        second = jnp.concatenate(
            [cube_ref[pl.ds(b + j, rank_one, stride=bi), :].astype(BF16) for j in range(wide_b)],
            axis=1,
        )
        seen = jnp.concatenate(
            [observed32_ref[pl.ds(b + j, bu, stride=bi), :] for j in range(wide_b)], axis=1
        )
        residual = (dot(user_rows, second, 1, 0) - seen).astype(BF16)
        back = dot(user_rows, residual, 0, 0)
        for j in range(wide_b):
            cube_ref[pl.ds(b + j, rank_one, stride=bi), :] = back[:, j * kc:(j + 1) * kc]
        return grad_user + dot(residual, second, 1, 1)

    grad_user = lax.fori_loop(0, bi // wide_b, middle, jnp.zeros((bu, rank_one), F32))
    user_out_ref[...] = jnp.zeros_like(user_out_ref)
    user_out_ref[pl.ds(user_start, bu), :] = grad_user * scale

    def backward(k, carry):
        grad_item, grad_ctx = carry
        start = pl.multiple_of(k * unit, unit)
        backs = [
            cube_ref[pl.ds(pl.multiple_of((k * across + j) * bi, bi), bi), :].astype(BF16)
            for j in range(across)
        ]
        firsts = [
            first_ref[pl.ds(pl.multiple_of(start + j * rank_two, rank_two), rank_two), :]
            for j in range(across)
        ]
        wide = jnp.concatenate(backs, axis=1)
        grad_item = grad_item + dot(wide, jnp.concatenate(firsts, axis=1), 1, 1)
        folded = dot(item_rows, wide, 0, 0).astype(BF16)
        folded = jnp.concatenate([folded[:, j * kc:(j + 1) * kc] for j in range(across)], axis=0)
        grad_ctx = grad_ctx + dot(folded, core_of(k), 0, 0)
        grad_core = (dot(folded, ctx_rows, 1, 0) * scale).astype(BF16)
        for j in range(per):
            terms_ref[k * per + j, pl.ds(0, m), :] = grad_core[j * m:(j + 1) * m]
        return grad_item, grad_ctx

    grad_item, grad_ctx = lax.fori_loop(
        0,
        total * m // unit,
        backward,
        (jnp.zeros((bi, rank_two), F32), jnp.zeros((kc, kc_rank), F32)),
    )
    terms_ref[:, pl.ds(item_at, up16(ni)), :] = jnp.zeros((total, up16(ni), rank_two), BF16)
    for j in range(bi // ni):
        piece = grad_item[j * ni:(j + 1) * ni] * scale
        if ni < up16(ni):
            piece = jnp.concatenate([piece, jnp.zeros((up16(ni) - ni, rank_two), F32)], axis=0)
        owner = (stratum * blocks + item_block) * (bi // ni) + j
        terms_ref[owner, pl.ds(item_at, up16(ni)), :] = piece.astype(BF16)
    grad_ctx = grad_ctx * scale
    high = grad_ctx.astype(BF16)
    low = (grad_ctx - high.astype(F32)).astype(BF16)
    spread = dot(picker, high, 1, 0) + dot(picker, low, 1, 0)
    terms_ref[:, pl.ds(ctx_at, ctx_pad), :] = spread.astype(BF16).reshape(total, ctx_pad, kc_rank)


def tile(sizes, index, ids, observed, everything, user_factor):
    bu, bi, kc = observed.shape
    total, rows, rank = everything.shape
    m = sizes[0]
    vmem = pl.BlockSpec(memory_space=pltpu.VMEM)
    cost = 9 * 2 * total * m * bi * kc
    return pl.pallas_call(
        functools.partial(tile_kernel, sizes),
        out_shape=(
            jax.ShapeDtypeStruct(everything.shape, BF16),
            jax.ShapeDtypeStruct(user_factor.shape, F32),
        ),
        in_specs=[pl.BlockSpec(memory_space=pltpu.SMEM)] + [vmem] * 4,
        out_specs=(vmem, vmem),
        scratch_shapes=[
            pltpu.VMEM((bu * bi, kc), F32),
            pltpu.VMEM((total * m, kc), BF16),
            pltpu.VMEM((total * m // rank * bi, kc), F32),
        ],
        compiler_params=pltpu.CompilerParams(vmem_limit_bytes=VMEM_LIMIT),
        cost_estimate=pl.CostEstimate(flops=cost, bytes_accessed=observed.size * 6, transcendentals=0),
        name="tile_gradients",
    )(index, ids, observed, everything, user_factor)


def scatter_kernel(
    grid, sizes, terms_ref, user_ref, core_out, item_out, ctx_out, user_out,
    c_in, keep, send_one, in_one, mid, send_two, in_two, send_three, in_three, user_in, total_ref,
    send_sems, recv_sems,
):
    m, ni, nk = sizes
    n = grid.n
    at = grid.here()
    rows = terms_ref.shape[1]
    enter(grid, at)
    wires = Wires(grid, send_sems, recv_sems)
    parts = [(part, *axes) for part, axes in zip(halves(rows), (("x", "y"), ("y", "x")))]
    both = n["x"] * n["y"]

    def spot(dx, dy):
        return dy * n["x"] + dx

    chunk = user_out.shape[0]
    user_copies = []
    for dx in range(1, n["x"]):
        to = grid.moved(at, x=dx)
        start = pl.multiple_of(to["x"] * chunk, chunk)
        user_copies.append(wires.start(user_ref.at[pl.ds(start, chunk)], user_in.at[dx - 1], to))

    zero = {}
    for dz in order(n["z"]):
        for dy in range(n["y"]):
            for dx in range(n["x"]):
                for dc in range(1, n["c"]):
                    to = grid.moved(at, z=dz, y=dy, x=dx, c=dc)
                    zero[dz, dy, dx, dc] = wires.start(
                        terms_ref.at[grid.shard(to)],
                        c_in.at[dc - 1, dz * both + spot(dx, dy)],
                        grid.moved(at, c=dc),
                    )
    one_copies, two_copies, three_copies = {}, {}, {}

    def stage_one(dz):
        for dy in range(n["y"]):
            for dx in range(n["x"]):
                for dc in range(1, n["c"]):
                    zero[dz, dy, dx, dc].wait_recv()
                own = grid.shard(grid.moved(at, z=dz, y=dy, x=dx))
                slot = dz * both + spot(dx, dy)
                for part, one, two in parts:
                    value = terms_ref[own, pl.ds(*part), :].astype(F32)
                    for dc in range(1, n["c"]):
                        value = value + c_in[dc - 1, slot, pl.ds(*part), :].astype(F32)
                    step = dx if one == "x" else dy
                    if not step:
                        keep[slot, pl.ds(*part), :] = value
                        continue
                    send_one[slot, pl.ds(*part), :] = value.astype(BF16)
                    one_copies[dz, dy, dx, part] = wires.start(
                        send_one.at[slot, pl.ds(*part)],
                        in_one.at[slot, pl.ds(*part)],
                        grid.moved(at, **{one: step}),
                    )

    def stage_two(dz):
        for part, one, two in parts:
            for d2 in range(n[two]):
                def steps(d1):
                    return (d1, d2) if one == "x" else (d2, d1)

                slot = dz * both + spot(*steps(0))
                value = keep[slot, pl.ds(*part), :]
                for d1 in range(1, n[one]):
                    dx, dy = steps(d1)
                    one_copies[dz, dy, dx, part].wait_recv()
                    value = value + in_one[dz * both + spot(dx, dy), pl.ds(*part), :].astype(F32)
                if not d2:
                    mid[dz, pl.ds(*part), :] = value
                    continue
                send_two[slot, pl.ds(*part), :] = value.astype(BF16)
                two_copies[dz, d2, part] = wires.start(
                    send_two.at[slot, pl.ds(*part)],
                    in_two.at[slot, pl.ds(*part)],
                    grid.moved(at, **{two: d2}),
                )

    def stage_three(dz):
        for part, one, two in parts:
            value = mid[dz, pl.ds(*part), :]
            for d2 in range(1, n[two]):
                dx, dy = (0, d2) if one == "x" else (d2, 0)
                two_copies[dz, d2, part].wait_recv()
                value = value + in_two[dz * both + spot(dx, dy), pl.ds(*part), :].astype(F32)
            if not dz:
                total_ref[pl.ds(*part), :] = value
                continue
            send_three[dz, pl.ds(*part), :] = value.astype(BF16)
            three_copies[dz, part] = wires.start(
                send_three.at[dz, pl.ds(*part)],
                in_three.at[dz, pl.ds(*part)],
                grid.moved(at, z=dz),
            )

    turns = order(n["z"])
    for k in range(len(turns) + 2):
        if k < len(turns):
            stage_one(turns[k])
        if 0 <= k - 1 < len(turns):
            stage_two(turns[k - 1])
        if 0 <= k - 2 < len(turns):
            stage_three(turns[k - 2])

    value = user_ref[pl.ds(pl.multiple_of(at["x"] * chunk, chunk), chunk), :]
    for dx, copy in enumerate(user_copies):
        copy.wait_recv()
        value = value + user_in[dx]
    user_out[...] = value
    for part, one, two in parts:
        value = total_ref[pl.ds(*part), :]
        for dz in range(1, n["z"]):
            three_copies[dz, part].wait_recv()
            value = value + in_three[dz, pl.ds(*part), :].astype(F32)
        total_ref[pl.ds(*part), :] = value
    core_out[...] = total_ref[pl.ds(0, m), :]
    item_out[...] = total_ref[pl.ds(m, ni), :]
    ctx_out[...] = total_ref[pl.ds(m + up16(ni), nk), :]
    wires.finish()


def scatter(grid, sizes, terms, term_user):
    m, ni, nk = sizes
    n = grid.n
    total, rows, rank = terms.shape
    chip = total // n["c"]
    chunk = term_user.shape[0] // n["x"]
    copies = 2 * total + n["x"]
    vmem = pl.BlockSpec(memory_space=pltpu.VMEM)
    plane = lambda count, kind: pltpu.VMEM((max(count, 1), rows, rank), kind)
    return pl.pallas_call(
        functools.partial(scatter_kernel, grid, sizes),
        out_shape=tuple(
            jax.ShapeDtypeStruct((count, rank), F32) for count in (m, ni, nk, chunk)
        ),
        in_specs=[vmem, vmem],
        out_specs=(vmem,) * 4,
        scratch_shapes=[
            pltpu.VMEM((max(n["c"] - 1, 1), chip, rows, rank), BF16),
            plane(chip, F32),
            plane(chip, BF16),
            plane(chip, BF16),
            plane(n["z"], F32),
            plane(chip, BF16),
            plane(chip, BF16),
            plane(n["z"], BF16),
            plane(n["z"], BF16),
            pltpu.VMEM((max(n["x"] - 1, 1), chunk, rank), F32),
            pltpu.VMEM((rows, rank), F32),
            pltpu.SemaphoreType.DMA((copies,)),
            pltpu.SemaphoreType.DMA((copies,)),
        ],
        compiler_params=pltpu.CompilerParams(
            collective_id=1, has_side_effects=True, vmem_limit_bytes=VMEM_LIMIT
        ),
        name="scatter_sums",
    )(terms, term_user)


def local(
    grid, observed, user_block, item_block, stratum, context_ids, core_tensor, user_factor,
    item_factor, context_factor,
):
    n = grid.n
    users, items = n["z"] * n["y"] * n["c"], n["x"]
    tiles_here, block_user, block_item, slices = observed.shape
    m = core_tensor.shape[0]
    ni = item_factor.shape[0] // users
    nk = context_factor.shape[0]
    rank = core_tensor.shape[1]
    scale = 1.0 / math.sqrt(block_user * block_item * slices)
    item_rows = lax.dynamic_slice_in_dim(item_factor, lax.axis_index("user") * ni, ni, 0)
    fill = lambda count: jnp.zeros((up16(count) - count, rank), BF16)
    shard = jnp.concatenate(
        [core_tensor.astype(BF16), item_rows, fill(ni), context_factor, fill(nk)], axis=0
    )
    everything = gather(grid, shard)
    sizes = (m, ni, nk, items, item_factor.shape[0] // block_item, scale)
    terms = term_user = None
    for t in range(tiles_here):
        index = jnp.stack([user_block[t], item_block[t], stratum[t]])
        one_terms, one_user = tile(
            sizes, index, context_ids[t:t + 1], observed[t], everything, user_factor
        )
        if t:
            terms = (terms.astype(F32) + one_terms.astype(F32)).astype(BF16)
            term_user = term_user + one_user
        else:
            terms, term_user = one_terms, one_user
    core_grad, item_grad, context_grad, user_grad = scatter(grid, (m, ni, nk), terms, term_user)
    return (core_grad, user_grad, item_grad, context_grad)


def solution(mesh):
    grid = Grid(mesh.shape["user"], mesh.shape["item"])
    both = ("user", "item")
    return jax.shard_map(
        functools.partial(local, grid),
        mesh=mesh,
        in_specs=(
            P(both, None, None, None),
            P(both),
            P(both),
            P(both),
            P(both, None),
            P(both, None),
            P("user", None),
            P("item", None),
            P(both, None),
        ),
        out_specs=(P(both, None), P(both, None), P(both, None), P(both, None)),
        check_vma=False,
    )
```

time: 394 us -> 142 us (0.36)
  waiting for transfers between devices: 232 us -> 0 us
  Pallas kernels: 0 us -> 130 us
  blocking collectives: 80.4 us -> 0 us
  matrix products: 49.5 us -> 0 us
  between operations: 16.9 us -> 2.64 us
  other arithmetic: 9.65 us -> 3.04 us
    reduce_scatter x6 -> x0, waiting for transfers between devices: 232 us -> none  [the longest x1 107 us: local(): lax.psum_scatter(term_core, 'user', scatter_dimension=0, tiled=True)]
    pallas_call x0 -> x3, Pallas kernels: none -> 130 us  [the longest x1 54.4 us: tile(): pl.pallas_call(functools.partial(tile_kernel, sizes), out_shape=(jax.Shap...]
    all_gather x2 -> x0, blocking collectives: 75.3 us -> none  [the longest x1 70.4 us: local(): lax.all_gather(context_factor, ('user', 'item'), axis=0, tiled=True)]
    dot_general x10 -> x0, matrix products: 49.5 us -> none  [the longest x1 18.2 us: tile_terms(): jnp.dot(user_rows, second_flat, preferred_element_type=jnp.float32)]
    unnamed x2 -> x0, other arithmetic: 6.51 us -> none
    unnamed x1 -> x0, blocking collectives: 5.1 us -> none
  transfers between devices with their start and end apart: 7 -> 0, of which waited for: 6 -> 0; matrix products, arithmetic and copies ran while one was open for 8% -> 0% of each run, Pallas kernels for 0% -> 0%
where the time goes in v1:
time: 142 us
  Pallas kernels  130 us (92%)
  local copies, waits for them, and re-layouts  5.89 us (4%)
  other arithmetic  3.04 us (2%)
  between operations  2.64 us (2%)
    pallas_call x1, Pallas kernels, tile(): pl.pallas_call(functools.partial(tile_kernel, sizes), out_shape=(jax.Shap...  54.4 us
    pallas_call x1, Pallas kernels, gather(): pl.pallas_call(functools.partial(gather_kernel, grid), out_shape=jax.Shap...  42.7 us
    pallas_call x1, Pallas kernels, scatter(): pl.pallas_call(functools.partial(scatter_kernel, grid, sizes), out_shape=...  32.9 us
    unnamed x6, local copies, waits for them, and re-layouts  5.81 us

profile of v1, /device:TPU:0, one launch (start us, length us, event | category | flops | bytes accessed | tf_op | source)
XLA Modules:
  0.0 141.6 jit_solution(2687043358905416120)
XLA Ops:
  0.6 0.0 copy-start
  2.6 0.6 pad_add_fusion.index_ref
  3.2 0.1 pad.3.clone
  3.3 0.0 copy-done
  3.3 1.0 convert_element_type.3
  4.3 1.5 %maximum_maximum_fusion.shard_ref = bf16[544,128]{1,0:T(8,128)(2,1)} fusion(bf16[8,128]{1,0:T(8,128)(2,1)} %param.17, bf16[16,128]{1,0:T(8,128)(2,1)S(1)} %constant_dynamic-slice_fusion, bf16[512,128]{1,0:T(8,128)(2,1)S(1)} %convert_element_type.3, bf16[544]{0:T(1024)(128)(2,1)S(1)} %pad.3.clone), kind=kLoop, calls=%fused_computation | loop fusion | flops 557056 | bytes 277568 | tf_op jit(solution)/shard_map/concatenate | solution.py:493
  5.7 42.7 %gather_factors.1.all_ref = bf16[32,544,128]{2,1,0:T(8,128)(2,1)} custom-call(bf16[544,128]{1,0:T(8,128)(2,1)} %maximum_maximum_fusion.shard_ref), custom_call_target="tpu_custom_call" | custom-call | tf_op jit(solution)/shard_map/gather_factors/pallas_call | solution.py:160
  48.5 54.4 %tile_gradients.1 = (bf16[32,544,128]{2,1,0:T(8,128)(2,1)}, f32[512,128]{1,0:T(8,128)}) custom-call(s32[3]{0:T(128)} %pad_add_fusion.index_ref, s32[1,128]{1,0:T(1,128)} %ids_ref.1, bf16[128,128,128]{2,1,0:T(8,128)(2,1)} %bitcast.1, bf16[32,544,128]{2,1,0:T(8,128)(2,1)} %gather_factors.1.all_ref, bf16[512,128]{1,0:T(8,128)(2,1)} %user_ref.1), custom_call_target="tpu_custom_call" | custom-call | flops 4831838208 | bytes 12582912 | tf_op jit(solution)/shard_map/tile_gradients/pallas_call | solution.py:298
  102.9 32.9 %scatter_sums.1 = (f32[512,128]{1,0:T(8,128)}, f32[16,128]{1,0:T(8,128)}, f32[8,128]{1,0:T(8,128)}, f32[256,128]{1,0:T(8,128)}) custom-call(bf16[32,544,128]{2,1,0:T(8,128)(2,1)} %get-tuple-element.10.terms_ref, f32[512,128]{1,0:T(8,128)} %get-tuple-element.11.user_ref), custom_call_target="tpu_custom_call" | custom-call | tf_op jit(solution)/shard_map/scatter_sums/pallas_call | solution.py:450
  135.8 1.7 %copy.20 = f32[512,128]{1,0:T(8,128)} copy(f32[512,128]{1,0:T(8,128)} %get-tuple-element.20) | data formatting | bytes 524288
  137.5 1.6 %copy.21 = f32[256,128]{1,0:T(8,128)} copy(f32[256,128]{1,0:T(8,128)} %get-tuple-element.21) | data formatting | bytes 262144
  139.0 1.3 copy.22
  140.3 1.3 copy.23
  (2 shorter events, 0.0 us)
Async XLA Ops:
  0.6 2.7 %copy-start = (bf16[256,128]{1,0:T(8,128)(2,1)S(1)}, bf16[256,128]{1,0:T(8,128)(2,1)}, u32[]{:S(2)}) copy-start(bf16[256,128]{1,0:T(8,128)(2,1)} %param.16) | copy-start | bytes 196612

commit v2 on v0

v2 whole, which is shorter than its diff:
```python
import functools
import math

import jax
import jax.numpy as jnp
from jax import lax
from jax.experimental import pallas as pl
from jax.experimental.pallas import tpu as pltpu
from jax.sharding import PartitionSpec as P

MESH = pl.DeviceIdType.MESH
F32 = jnp.float32
BF16 = jnp.bfloat16
VMEM_LIMIT = 60 * 1024 * 1024


def up16(rows):
    return (rows + 15) // 16 * 16


def dot(left, right, left_dim, right_dim):
    return lax.dot_general(
        left, right, (((left_dim,), (right_dim,)), ((), ())), preferred_element_type=F32
    )


class Grid:
    def __init__(self, users, items):
        nc = 2 if users % 2 == 0 else 1
        rest = users // nc
        ny = 1
        while rest % (2 * ny) == 0 and (2 * ny) * (2 * ny) <= rest:
            ny *= 2
        self.n = {"z": rest // ny, "y": ny, "c": nc, "x": items}

    def here(self):
        user = lax.axis_index("user")
        n = self.n
        return {
            "c": lax.rem(user, n["c"]),
            "y": lax.rem(lax.div(user, n["c"]), n["y"]),
            "z": lax.div(user, n["c"] * n["y"]),
            "x": lax.axis_index("item"),
        }

    def moved(self, at, **steps):
        out = dict(at)
        for axis, step in steps.items():
            if step:
                out[axis] = lax.rem(at[axis] + step + self.n[axis], self.n[axis])
        return out

    def device(self, at):
        n = self.n
        return ((at["z"] * n["y"] + at["y"]) * n["c"] + at["c"], at["x"])

    def shard(self, at):
        user, item = self.device(at)
        return user * self.n["x"] + item

    def partners(self, at):
        return [
            self.moved(at, **{axis: step})
            for axis in "zycx"
            for step in range(1, self.n[axis])
        ]


def enter(grid, at):
    barrier = pltpu.get_barrier_semaphore()
    others = grid.partners(at)
    for other in others:
        pl.semaphore_signal(barrier, inc=1, device_id=grid.device(other), device_id_type=MESH)
    pl.semaphore_wait(barrier, len(others))


class Wires:
    def __init__(self, grid, send_sems, recv_sems):
        self.grid, self.send, self.recv, self.used, self.copies = grid, send_sems, recv_sems, 0, []

    def start(self, src, dst, to):
        copy = pltpu.make_async_remote_copy(
            src_ref=src,
            dst_ref=dst,
            send_sem=self.send.at[self.used],
            recv_sem=self.recv.at[self.used],
            device_id=self.grid.device(to),
            device_id_type=MESH,
        )
        copy.start()
        self.used += 1
        self.copies.append(copy)
        return copy

    def finish(self):
        for copy in self.copies:
            copy.wait_send()


def halves(rows):
    first = up16(rows // 2)
    return (0, first), (first, rows - first)


def order(n):
    return [(step + 1) % n for step in range(n)]


class GatherFlow:
    def __init__(self, wires, grid, at, ref, part, one, two):
        self.wires, self.grid, self.at, self.ref = wires, grid, at, ref
        self.part, self.one, self.two = part, one, two
        self.z, self.first, self.second, self.core = {}, {}, {}, {}

    def send(self, owner, **to):
        ref = self.ref.at[self.grid.shard(owner), pl.ds(*self.part)]
        return self.wires.start(ref, ref, self.grid.moved(self.at, **to))

    def start(self):
        for dz in range(1, self.grid.n["z"]):
            self.z[dz] = self.send(self.at, z=dz)

    def stage_one(self, dz):
        if dz:
            self.z[dz].wait_recv()
        owner = self.grid.moved(self.at, z=-dz)
        for d1 in range(1, self.grid.n[self.one]):
            self.first[dz, d1] = self.send(owner, **{self.one: d1})

    def stage_two(self, dz):
        for d1 in range(self.grid.n[self.one]):
            if d1:
                self.first[dz, d1].wait_recv()
            owner = self.grid.moved(self.at, **{"z": -dz, self.one: -d1})
            for d2 in range(1, self.grid.n[self.two]):
                self.second[dz, d1, d2] = self.send(owner, **{self.two: d2})

    def stage_core(self, dz):
        for d1 in range(self.grid.n[self.one]):
            for d2 in range(self.grid.n[self.two]):
                if d2:
                    self.second[dz, d1, d2].wait_recv()
                owner = self.grid.moved(self.at, **{"z": -dz, self.one: -d1, self.two: -d2})
                for dc in range(1, self.grid.n["c"]):
                    self.core[dz, d1, d2, dc] = self.send(owner, c=dc)

    def end(self, dz, dc):
        for key, copy in self.core.items():
            if key[0] == dz and key[3] == dc:
                copy.wait_recv()


class ScatterFlow:
    def __init__(self, wires, grid, at, terms, part, one, two, planes):
        self.wires, self.grid, self.at, self.terms = wires, grid, at, terms
        self.part, self.one, self.two, self.planes = part, one, two, planes
        self.core, self.first, self.second, self.z = {}, {}, {}, {}

    def rows(self):
        return pl.ds(*self.part)

    def slot(self, dz, d1, d2):
        n = self.grid.n
        return (dz * n[self.one] + d1) * n[self.two] + d2

    def send(self, name, target, slot, value, **to):
        rows = self.rows()
        self.planes["send_" + name][slot, rows, :] = value.astype(BF16)
        return self.wires.start(
            self.planes["send_" + name].at[slot, rows],
            self.planes["in_" + name].at[slot, rows],
            self.grid.moved(self.at, **to),
        )

    def got(self, name, slot):
        return self.planes["in_" + name][slot, self.rows(), :].astype(F32)

    def each(self):
        n = self.grid.n
        return [(d1, d2) for d1 in range(n[self.one]) for d2 in range(n[self.two])]

    def start(self, dz):
        chip = self.grid.n["z"] * len(self.each())
        for d1, d2 in self.each():
            for dc in range(1, self.grid.n["c"]):
                steps = {"z": dz, self.one: d1, self.two: d2, "c": dc}
                self.core[dz, d1, d2, dc] = self.wires.start(
                    self.terms.at[self.grid.shard(self.grid.moved(self.at, **steps)), self.rows()],
                    self.planes["in_c"].at[(dc - 1) * chip + self.slot(dz, d1, d2), self.rows()],
                    self.grid.moved(self.at, c=dc),
                )

    def stage_one(self, dz):
        chip = self.grid.n["z"] * len(self.each())
        for d1, d2 in reversed(self.each()):
            slot = self.slot(dz, d1, d2)
            own = self.grid.shard(self.grid.moved(self.at, **{"z": dz, self.one: d1, self.two: d2}))
            value = self.terms[own, self.rows(), :].astype(F32)
            for dc in range(1, self.grid.n["c"]):
                self.core[dz, d1, d2, dc].wait_recv()
                value = value + self.got("c", (dc - 1) * chip + slot)
            if d1:
                self.first[dz, d1, d2] = self.send("one", d1, slot, value, **{self.one: d1})
            else:
                self.planes["keep"][dz * self.grid.n[self.two] + d2, self.rows(), :] = value

    def stage_two(self, dz):
        for d2 in reversed(range(self.grid.n[self.two])):
            slot = dz * self.grid.n[self.two] + d2
            value = self.planes["keep"][slot, self.rows(), :]
            for d1 in range(1, self.grid.n[self.one]):
                self.first[dz, d1, d2].wait_recv()
                value = value + self.got("one", self.slot(dz, d1, d2))
            if d2:
                self.second[dz, d2] = self.send("two", d2, slot, value, **{self.two: d2})
            else:
                self.planes["mid"][dz, self.rows(), :] = value

    def stage_three(self, dz):
        value = self.planes["mid"][dz, self.rows(), :]
        for d2 in range(1, self.grid.n[self.two]):
            self.second[dz, d2].wait_recv()
            value = value + self.got("two", dz * self.grid.n[self.two] + d2)
        if dz:
            self.z[dz] = self.send("z", dz, dz, value, z=dz)
        else:
            self.planes["mid"][dz, self.rows(), :] = value

    def end(self):
        value = self.planes["mid"][0, self.rows(), :]
        for dz in range(1, self.grid.n["z"]):
            self.z[dz].wait_recv()
            value = value + self.got("z", dz)
        return value


PLANES = ("in_c", "keep", "send_one", "in_one", "mid", "send_two", "in_two", "send_z", "in_z")


def planes_for(grid, rows, rank):
    n = grid.n
    chip, most = n["z"] * n["y"] * n["x"], n["z"] * max(n["x"], n["y"])
    counts = {
        "in_c": chip * max(n["c"] - 1, 1),
        "send_one": chip,
        "in_one": chip,
        "keep": most,
        "send_two": most,
        "in_two": most,
        "mid": n["z"],
        "send_z": n["z"],
        "in_z": n["z"],
    }
    kind = lambda name: F32 if name in ("keep", "mid") else BF16
    return [pltpu.VMEM((counts[name], rows, rank), kind(name)) for name in PLANES]


def whole_kernel(
    grid, scale,
    user_block_ref, item_block_ref, stratum_ref, ids_ref, observed_hbm, core_ref, user_ref, item_ref,
    context_ref,
    core_out, item_out, ctx_out, user_out,
    observed_ref, wide_ref, item32_ref, cores_ref, first_ref, cube_ref, few_ref, few_terms_ref,
    user_terms_ref, user_in, *rest,
):
    count = len(PLANES)
    big = dict(zip(PLANES, rest[:count]))
    little = dict(zip(PLANES, rest[count:2 * count]))
    load_sem, send_sems, recv_sems = rest[2 * count:]
    n = grid.n
    at = grid.here()
    total, m, rank = cores_ref.shape
    bu, bi, kc = observed_ref.shape
    users = total // n["x"]
    ni, nk = item_ref.shape[0] // users, context_ref.shape[0]
    ni_pad, nk_pad = up16(ni), up16(nk)
    rank_two = rank
    rank_one = total * m // rank_two
    pitch = bi + 8
    group = n["x"] * m
    across = group // rank_two

    load = pltpu.make_async_copy(observed_hbm, observed_ref, load_sem)
    load.start()
    own = grid.shard(at)
    cores_ref[own] = core_ref[...].astype(BF16)
    item32_ref[...] = item_ref[...].astype(F32)
    start = pl.multiple_of(grid.device(at)[0] * ni, ni)

    def padded(value, rows):
        if value.shape[0] == rows:
            return value.astype(BF16)
        fill = jnp.zeros((rows - value.shape[0], rank), F32)
        return jnp.concatenate([value, fill], axis=0).astype(BF16)

    few_ref[own, pl.ds(0, ni_pad), :] = padded(item32_ref[pl.ds(start, ni), :], ni_pad)
    few_ref[own, pl.ds(ni_pad, nk_pad), :] = padded(context_ref[...].astype(F32), nk_pad)
    enter(grid, at)
    wires = Wires(grid, send_sems, recv_sems)
    low, high = halves(m)
    few_part = (0, ni_pad + nk_pad)
    few = GatherFlow(wires, grid, at, few_ref, few_part, "y", "x")
    flows = [
        GatherFlow(wires, grid, at, cores_ref, low, "y", "x"),
        GatherFlow(wires, grid, at, cores_ref, high, "x", "y"),
    ]
    few.start()
    few.stage_one(0)
    for flow in flows:
        flow.start()
    for flow in flows:
        flow.stage_one(0)
    for dz in range(1, n["z"]):
        few.stage_one(dz)
    load.wait()

    def widen(a, carry):
        row = pl.multiple_of(a * pitch, 8)
        wide_ref[pl.ds(row, bi), :] = observed_ref[a].astype(F32)
        return carry

    lax.fori_loop(0, bu, widen, 0, unroll=4)
    for dz in range(n["z"]):
        few.stage_two(dz)
    for flow in flows:
        flow.stage_two(0)
    for dz in range(n["z"]):
        few.stage_core(dz)
    if n["z"] > 1:
        for flow in flows:
            flow.stage_one(1)
    for dz in range(n["z"]):
        for dc in range(1, n["c"]):
            few.end(dz, dc)

    user_block, item_block, stratum = user_block_ref[0], item_block_ref[0], stratum_ref[0]
    blocks = item_ref.shape[0] // bi
    chosen = jnp.full((bu, rank), user_block, jnp.int32)
    user32 = jnp.zeros((bu, rank), F32)
    for j in range(user_ref.shape[0] // bu):
        user32 = jnp.where(chosen == j, user_ref[pl.ds(j * bu, bu), :].astype(F32), user32)
    user_rows, user_turned = user32.astype(BF16), user32.T.astype(BF16)
    chosen = jnp.full((bi, rank), stratum * blocks + item_block, jnp.int32)
    item32 = jnp.zeros((bi, rank), F32)
    for block in range(n["x"] * blocks):
        begin = (block % blocks) * (bi // ni) * n["x"] + block // blocks
        rows = jnp.concatenate(
            [
                few_ref[begin + j * n["x"], pl.ds(0, ni_pad), :].astype(F32)[:ni]
                for j in range(bi // ni)
            ],
            axis=0,
        )
        item32 = jnp.where(chosen == block, rows, item32)
    item_rows, item_turned = item32.astype(BF16), item32.T.astype(BF16)
    ids = ids_ref[...]
    places = lax.div(ids, jnp.full_like(ids, nk)) * nk_pad + lax.rem(ids, jnp.full_like(ids, nk))
    spots = lax.broadcasted_iota(jnp.int32, (total * nk_pad, kc), 0)
    picker = jnp.where(spots == places, 1.0, 0.0).astype(BF16)
    ctx_all = few_ref[:, pl.ds(ni_pad, nk_pad), :].reshape(total * nk_pad, rank)
    ctx32 = dot(picker, ctx_all, 0, 0)
    ctx_rows, ctx_turned = ctx32.astype(BF16), ctx32.T.astype(BF16)

    def first_shard(dz, dy, dc):
        z = lax.rem(at["z"] + dz + n["z"], n["z"])
        y = lax.rem(at["y"] + dy, n["y"])
        c = lax.rem(at["c"] + dc, n["c"])
        return ((z * n["y"] + y) * n["c"] + c) * n["x"]

    def forward(dz, dc):
        def step(dy, carry):
            shard = first_shard(-dz, dy, dc)
            core = cores_ref[pl.ds(shard, n["x"]), :, :].reshape(group, rank)
            first = dot(core, ctx_turned, 1, 0).astype(BF16)
            row = pl.multiple_of(shard * m, group)
            first_ref[pl.ds(row, group), :] = first
            wide = jnp.concatenate(
                [first[j * rank_two:(j + 1) * rank_two] for j in range(across)], axis=1
            )
            second = dot(item_rows, wide, 1, 0)
            p = lax.div(shard * m, rank_two)
            for j in range(across):
                cube_ref[pl.ds(pl.multiple_of((p + j) * pitch, 8), bi), :] = (
                    second[:, j * kc:(j + 1) * kc]
                )
            return carry

        lax.fori_loop(0, n["y"], step, 0)

    last = n["z"] - 1
    for k in range(n["z"] + 3):
        if 2 <= k <= last:
            for flow in flows:
                flow.stage_one(k)
        if 1 <= k - 1 <= last:
            for flow in flows:
                flow.stage_two(k - 1)
        if 0 <= k - 2 <= last:
            for flow in flows:
                flow.stage_core(k - 2)
            forward(k - 2, 0)
        if 0 <= k - 3 <= last:
            for dc in range(1, n["c"]):
                for flow in flows:
                    flow.end(k - 3, dc)
                forward(k - 3, dc)

    wide_b = 8

    def middle(k, grad_user):
        b = k * wide_b
        second = jnp.concatenate(
            [cube_ref[pl.ds(b + j, rank_one, stride=pitch), :].astype(BF16) for j in range(wide_b)],
            axis=1,
        )
        seen = jnp.concatenate(
            [wide_ref[pl.ds(b + j, bu, stride=pitch), :] for j in range(wide_b)], axis=1
        )
        residual = (dot(user_rows, second, 1, 0) - seen).astype(BF16)
        back = dot(user_turned, residual, 1, 0)
        for j in range(wide_b):
            cube_ref[pl.ds(b + j, rank_one, stride=pitch), :] = back[:, j * kc:(j + 1) * kc]
        return grad_user + dot(residual, second, 1, 1)

    grad_user = lax.fori_loop(0, bi // wide_b, middle, jnp.zeros((bu, rank_one), F32))
    grad_user = grad_user * scale
    for j in range(user_ref.shape[0] // bu):
        here = jnp.full(grad_user.shape, user_block, jnp.int32) == j
        user_terms_ref[pl.ds(j * bu, bu), :] = jnp.where(here, grad_user, 0.0)
    wires.finish()
    wires.copies = []

    chunk = user_out.shape[0]
    user_copies = []
    for dx in range(1, n["x"]):
        to = grid.moved(at, x=dx)
        start = pl.multiple_of(to["x"] * chunk, chunk)
        user_copies.append(
            wires.start(user_terms_ref.at[pl.ds(start, chunk)], user_in.at[dx - 1], to)
        )

    sums = [
        ScatterFlow(wires, grid, at, cores_ref, low, "x", "y", big),
        ScatterFlow(wires, grid, at, cores_ref, high, "y", "x", big),
    ]

    def backward(dz, dc, carry):
        def step(dy, carry):
            grad_item, grad_ctx = carry
            shard = first_shard(dz, dy, dc)
            p = lax.div(shard * m, rank_two)
            row = pl.multiple_of(shard * m, group)
            core = cores_ref[pl.ds(shard, n["x"]), :, :].reshape(group, rank)
            wide = jnp.concatenate(
                [
                    cube_ref[pl.ds(pl.multiple_of((p + j) * pitch, 8), bi), :].astype(BF16)
                    for j in range(across)
                ],
                axis=1,
            )
            first = first_ref[pl.ds(row, group), :]
            first = jnp.concatenate(
                [first[j * rank_two:(j + 1) * rank_two] for j in range(across)], axis=1
            )
            grad_item = grad_item + dot(wide, first, 1, 1)
            folded = dot(item_turned, wide, 1, 0).astype(BF16)
            folded = jnp.concatenate(
                [folded[:, j * kc:(j + 1) * kc] for j in range(across)], axis=0
            )
            grad_ctx = grad_ctx + dot(folded, core, 0, 0)
            grad_core = (dot(folded, ctx_rows, 1, 0) * scale).astype(BF16)
            cores_ref[pl.ds(shard, n["x"]), :, :] = grad_core.reshape(n["x"], m, rank)
            return grad_item, grad_ctx

        return lax.fori_loop(0, n["y"], step, carry)

    carry = (jnp.zeros((bi, rank_two), F32), jnp.zeros((kc, rank), F32))
    turns = order(n["z"])
    for k, dz in enumerate(turns):
        for dc in range(1, n["c"]):
            carry = backward(dz, dc, carry)
        for flow in sums:
            flow.start(dz)
        carry = backward(dz, 0, carry)
        if k + 1 < len(turns):
            for flow in sums:
                flow.stage_one(dz)
        if k >= 1:
            for flow in sums:
                flow.stage_two(turns[k - 1])
        if k >= 2:
            for flow in sums:
                flow.stage_three(turns[k - 2])

    grad_item, grad_ctx = carry
    grad_item, grad_ctx = grad_item * scale, grad_ctx * scale
    mine = jnp.full((ni_pad, rank), stratum * blocks + item_block, jnp.int32)
    for block in range(n["x"] * blocks):
        for j in range(bi // ni):
            piece = padded(grad_item[j * ni:(j + 1) * ni], ni_pad).astype(F32)
            few_terms_ref[block * (bi // ni) + j, pl.ds(0, ni_pad), :] = (
                jnp.where(mine == block, piece, 0.0).astype(BF16)
            )
    upper = grad_ctx.astype(BF16)
    lower = (grad_ctx - upper.astype(F32)).astype(BF16)
    spread = dot(picker, upper, 1, 0) + dot(picker, lower, 1, 0)
    few_terms_ref[:, pl.ds(ni_pad, nk_pad), :] = spread.astype(BF16).reshape(total, nk_pad, rank)
    few_sums = ScatterFlow(wires, grid, at, few_terms_ref, few_part, "x", "y", little)
    for dz in turns:
        few_sums.start(dz)
    for flow in sums:
        flow.stage_one(turns[-1])
    for dz in turns:
        few_sums.stage_one(dz)
    for flow in sums:
        flow.stage_two(turns[-1])
    if len(turns) >= 2:
        for flow in sums:
            flow.stage_three(turns[-2])
    for dz in turns:
        few_sums.stage_two(dz)
    for flow in sums:
        flow.stage_three(turns[-1])
    for dz in turns:
        few_sums.stage_three(dz)

    value = user_terms_ref[pl.ds(pl.multiple_of(at["x"] * chunk, chunk), chunk), :]
    for dx, copy in enumerate(user_copies):
        copy.wait_recv()
        value = value + user_in[dx]
    user_out[...] = value
    for flow in sums:
        core_out[pl.ds(*flow.part), :] = flow.end()
    value = few_sums.end()
    item_out[...] = value[:ni]
    ctx_out[...] = value[ni_pad:ni_pad + nk]
    wires.finish()


def whole(grid, scale, user_block, item_block, stratum, ids, observed, core, users, items, contexts):
    n = grid.n
    total = n["z"] * n["y"] * n["c"] * n["x"]
    bu, bi, kc = observed.shape
    m, rank = core.shape
    ni, nk = items.shape[0] // (total // n["x"]), contexts.shape[0]
    few = up16(ni) + up16(nk)
    chunk = users.shape[0] // n["x"]
    copies = 6 * total + n["x"]
    pitch = bi + 8
    vmem, smem = pl.BlockSpec(memory_space=pltpu.VMEM), pl.BlockSpec(memory_space=pltpu.SMEM)
    return pl.pallas_call(
        functools.partial(whole_kernel, grid, scale),
        out_shape=tuple(
            jax.ShapeDtypeStruct((count, rank), F32) for count in (m, ni, nk, chunk)
        ),
        in_specs=[smem] * 3 + [vmem, pl.BlockSpec(memory_space=pl.ANY)] + [vmem] * 4,
        out_specs=(vmem,) * 4,
        scratch_shapes=[
            pltpu.VMEM((bu, bi, kc), BF16),
            pltpu.VMEM((bu * pitch, kc), F32),
            pltpu.VMEM(items.shape, F32),
            pltpu.VMEM((total, m, rank), BF16),
            pltpu.VMEM((total * m, kc), BF16),
            pltpu.VMEM((total * m // rank * pitch, kc), F32),
            pltpu.VMEM((total, few, rank), BF16),
            pltpu.VMEM((total, few, rank), BF16),
            pltpu.VMEM(users.shape, F32),
            pltpu.VMEM((max(n["x"] - 1, 1), chunk, rank), F32),
            *planes_for(grid, m, rank),
            *planes_for(grid, few, rank),
            pltpu.SemaphoreType.DMA,
            pltpu.SemaphoreType.DMA((copies,)),
            pltpu.SemaphoreType.DMA((copies,)),
        ],
        compiler_params=pltpu.CompilerParams(
            collective_id=0, has_side_effects=True, vmem_limit_bytes=VMEM_LIMIT
        ),
        cost_estimate=pl.CostEstimate(
            flops=9 * 2 * total * m * bi * kc, bytes_accessed=observed.size * 2, transcendentals=0
        ),
        name="tucker_gradient",
    )(user_block, item_block, stratum, ids, observed, core, users, items, contexts)


def hand_over_kernel(*refs):
    half = len(refs) // 2
    for source, target in zip(refs[:half], refs[half:]):
        target[...] = source[...]


def hand_over(arrays):
    vmem = pl.BlockSpec(memory_space=pltpu.VMEM)
    return pl.pallas_call(
        hand_over_kernel,
        out_shape=tuple(jax.ShapeDtypeStruct(a.shape, a.dtype) for a in arrays),
        in_specs=[vmem] * len(arrays),
        out_specs=(vmem,) * len(arrays),
        name="hand_over",
    )(*arrays)


def local(
    grid, observed, user_block, item_block, stratum, context_ids, core_tensor, user_factor,
    item_factor, context_factor,
):
    tiles_here, block_user, block_item, slices = observed.shape
    scale = 1.0 / math.sqrt(block_user * block_item * slices)
    sums = None
    for t in range(tiles_here):
        one = slice(t, t + 1)
        terms = whole(
            grid, scale, user_block[one], item_block[one], stratum[one], context_ids[one],
            observed[t], core_tensor, user_factor, item_factor, context_factor,
        )
        sums = terms if sums is None else tuple(a + b for a, b in zip(sums, terms))
    core_grad, item_grad, context_grad, user_grad = hand_over(sums)
    return (core_grad, user_grad, item_grad, context_grad)


def solution(mesh):
    grid = Grid(mesh.shape["user"], mesh.shape["item"])
    both = ("user", "item")
    return jax.shard_map(
        functools.partial(local, grid),
        mesh=mesh,
        in_specs=(
            P(both, None, None, None),
            P(both),
            P(both),
            P(both),
            P(both, None),
            P(both, None),
            P("user", None),
            P("item", None),
            P(both, None),
        ),
        out_specs=(P(both, None), P(both, None), P(both, None), P(both, None)),
        check_vma=False,
    )
```

time: 394 us -> 82.3 us (0.21)
  waiting for transfers between devices: 232 us -> 0 us
  blocking collectives: 80.4 us -> 0 us
  Pallas kernels: 0 us -> 79.5 us
  matrix products: 49.5 us -> 0 us
  between operations: 16.9 us -> 2.58 us
  other arithmetic: 9.65 us -> 0 us
  local copies, waits for them, and re-layouts: 4.72 us -> 0 us
    reduce_scatter x6 -> x0, waiting for transfers between devices: 232 us -> none  [the longest x1 107 us: local(): lax.psum_scatter(term_core, 'user', scatter_dimension=0, tiled=True)]
    pallas_call x0 -> x2, Pallas kernels: none -> 79.5 us  [the longest x1 77.8 us: whole(): pl.pallas_call(functools.partial(whole_kernel, grid, scale), out_shape=tu...]
    all_gather x2 -> x0, blocking collectives: 75.3 us -> none  [the longest x1 70.4 us: local(): lax.all_gather(context_factor, ('user', 'item'), axis=0, tiled=True)]
    dot_general x10 -> x0, matrix products: 49.5 us -> none  [the longest x1 18.2 us: tile_terms(): jnp.dot(user_rows, second_flat, preferred_element_type=jnp.float32)]
    unnamed x2 -> x0, other arithmetic: 6.51 us -> none
    unnamed x1 -> x0, blocking collectives: 5.1 us -> none
    unnamed x21 -> x0, local copies, waits for them, and re-layouts: 3.98 us -> none
  transfers between devices with their start and end apart: 7 -> 0, of which waited for: 6 -> 0; matrix products, arithmetic and copies ran while one was open for 8% -> 0% of each run, Pallas kernels for 0% -> 0%
where the time goes in v2:
time: 82.3 us; the launch traced here: 82.1 us
  Pallas kernels  79.5 us (97%)
  between operations  2.58 us (3%)
    pallas_call x1, Pallas kernels, whole(): pl.pallas_call(functools.partial(whole_kernel, grid, scale), out_shape=tu...  77.8 us
    pallas_call x1, Pallas kernels, hand_over(): pl.pallas_call(hand_over_kernel, out_shape=tuple((jax.ShapeDtypeStruct(a....  1.77 us

profile of v2, /device:TPU:0, one launch (start us, length us, event | category | flops | bytes accessed | tf_op | source)
XLA Modules:
  0.0 82.1 jit_solution(3995252477031973538)
XLA Ops:
  2.6 77.8 %tucker_gradient.1 = (f32[512,128]{1,0:T(8,128)}, f32[16,128]{1,0:T(8,128)}, f32[8,128]{1,0:T(8,128)}, f32[256,128]{1,0:T(8,128)}) custom-call(s32[1]{0:T(128)S(6)} %copy.13.user_block_ref, s32[1]{0:T(128)S(6)} %copy.14.item_block_ref, s32[1]{0:T(128)S(6)} %copy.15.stratum_ref, s32[1,128]{1,0:T(1,128)} %ids_ref.1, bf16[128,128,128]{2,1,0:T(8,128)(2,1)} %bitcast.1, ...), custom_call_target="tpu_custom_call" | custom-call | flops 4831838208 | bytes 4194304 | tf_op jit(solution)/shard_map/tucker_gradient/pallas_call | solution.py:551
  80.3 1.8 %hand_over.1 = (f32[512,128]{1,0:T(8,128)}, f32[16,128]{1,0:T(8,128)}, f32[8,128]{1,0:T(8,128)}, f32[256,128]{1,0:T(8,128)}) custom-call(f32[512,128]{1,0:T(8,128)} %get-tuple-element.12.refs_0_, f32[16,128]{1,0:T(8,128)} %get-tuple-element.13.refs_1_, f32[8,128]{1,0:T(8,128)} %get-tuple-element.14.refs_2_, f32[256,128]{1,0:T(8,128)} %get-tuple-element.15.refs_3_), custom_call_target="tpu_custom_call" | custom-call | tf_op jit(solution)/shard_map/hand_over/pallas_call | solution.py:593

commit v3 on v2

--- a/solution.py
+++ b/solution.py
@@ -304,31 +304,39 @@
         GatherFlow(wires, grid, at, cores_ref, low, "y", "x"),
         GatherFlow(wires, grid, at, cores_ref, high, "x", "y"),
     ]
+    last = n["z"] - 1
+
+    def each(stage, dz):
+        if dz <= last:
+            for flow in flows:
+                getattr(flow, stage)(dz)
+
     few.start()
     few.stage_one(0)
     for flow in flows:
         flow.start()
-    for flow in flows:
-        flow.stage_one(0)
+    each("stage_one", 0)
     for dz in range(1, n["z"]):
         few.stage_one(dz)
-    load.wait()
-
-    def widen(a, carry):
-        row = pl.multiple_of(a * pitch, 8)
-        wide_ref[pl.ds(row, bi), :] = observed_ref[a].astype(F32)
-        return carry
-
-    lax.fori_loop(0, bu, widen, 0, unroll=4)
+    each("stage_two", 0)
     for dz in range(n["z"]):
         few.stage_two(dz)
-    for flow in flows:
-        flow.stage_two(0)
+    each("stage_one", 1)
     for dz in range(n["z"]):
         few.stage_core(dz)
-    if n["z"] > 1:
-        for flow in flows:
-            flow.stage_one(1)
+    each("stage_core", 0)
+    each("stage_two", 1)
+    load.wait()
+
+    def widen(quarter):
+        def step(a, carry):
+            row = pl.multiple_of(a * pitch, 8)
+            wide_ref[pl.ds(row, bi), :] = observed_ref[a].astype(F32)
+            return carry
+
+        lax.fori_loop(bu * quarter // n["z"], bu * (quarter + 1) // n["z"], step, 0, unroll=4)
+
+    widen(0)
     for dz in range(n["z"]):
         for dc in range(1, n["c"]):
             few.end(dz, dc)
@@ -387,23 +395,17 @@
 
         lax.fori_loop(0, n["y"], step, 0)
 
-    last = n["z"] - 1
-    for k in range(n["z"] + 3):
-        if 2 <= k <= last:
+    for k in range(2, n["z"] + 2):
+        each("stage_one", k)
+        forward(k - 2, 0)
+        each("stage_two", k)
+        each("stage_core", k - 1)
+        if k - 1 <= last:
+            widen(k - 1)
+        for dc in range(1, n["c"]):
             for flow in flows:
-                flow.stage_one(k)
-        if 1 <= k - 1 <= last:
-            for flow in flows:
-                flow.stage_two(k - 1)
-        if 0 <= k - 2 <= last:
-            for flow in flows:
-                flow.stage_core(k - 2)
-            forward(k - 2, 0)
-        if 0 <= k - 3 <= last:
-            for dc in range(1, n["c"]):
-                for flow in flows:
-                    flow.end(k - 3, dc)
-                forward(k - 3, dc)
+                flow.end(k - 2, dc)
+            forward(k - 2, dc)
 
     wide_b = 8
 
@@ -481,16 +483,15 @@
             carry = backward(dz, dc, carry)
         for flow in sums:
             flow.start(dz)
-        carry = backward(dz, 0, carry)
-        if k + 1 < len(turns):
-            for flow in sums:
-                flow.stage_one(dz)
         if k >= 1:
             for flow in sums:
                 flow.stage_two(turns[k - 1])
-        if k >= 2:
+        carry = backward(dz, 0, carry)
+        for flow in sums:
+            flow.stage_one(dz)
+        if k >= 1:
             for flow in sums:
-                flow.stage_three(turns[k - 2])
+                flow.stage_three(turns[k - 1])
 
     grad_item, grad_ctx = carry
     grad_item, grad_ctx = grad_item * scale, grad_ctx * scale
@@ -509,18 +510,13 @@
     for dz in turns:
         few_sums.start(dz)
     for flow in sums:
-        flow.stage_one(turns[-1])
+        flow.stage_two(turns[-1])
     for dz in turns:
         few_sums.stage_one(dz)
     for flow in sums:
-        flow.stage_two(turns[-1])
-    if len(turns) >= 2:
-        for flow in sums:
-            flow.stage_three(turns[-2])
+        flow.stage_three(turns[-1])
     for dz in turns:
         few_sums.stage_two(dz)
-    for flow in sums:
-        flow.stage_three(turns[-1])
     for dz in turns:
         few_sums.stage_three(dz)
 

time: 82.3 us -> 92.1 us (1.12)
  Pallas kernels: 79.5 us -> 89.4 us
    pallas_call x1, Pallas kernels: 77.8 us -> 87.6 us  [whole(): pl.pallas_call(functools.partial(whole_kernel, grid, scale), out_shape=tu...]
where the time goes in v3:
time: 92.1 us; the launch traced here: 92 us
  Pallas kernels  89.4 us (97%)
  between operations  2.58 us (3%)
    pallas_call x1, Pallas kernels, whole(): pl.pallas_call(functools.partial(whole_kernel, grid, scale), out_shape=tu...  87.6 us

profile of v3, /device:TPU:0, one launch (start us, length us, event | category | flops | bytes accessed | tf_op | source)
XLA Modules:
  0.0 92.0 jit_solution(292476925181502244)
XLA Ops:
  2.6 87.6 %tucker_gradient.1 = (f32[512,128]{1,0:T(8,128)}, f32[16,128]{1,0:T(8,128)}, f32[8,128]{1,0:T(8,128)}, f32[256,128]{1,0:T(8,128)}) custom-call(s32[1]{0:T(128)S(6)} %copy.13.user_block_ref, s32[1]{0:T(128)S(6)} %copy.14.item_block_ref, s32[1]{0:T(128)S(6)} %copy.15.stratum_ref, s32[1,128]{1,0:T(1,128)} %ids_ref.1, bf16[128,128,128]{2,1,0:T(8,128)(2,1)} %bitcast.1, ...), custom_call_target="tpu_custom_call" | custom-call | flops 4831838208 | bytes 4194304 | tf_op jit(solution)/shard_map/tucker_gradient/pallas_call | solution.py:547
  90.2 1.8 %hand_over.1 = (f32[512,128]{1,0:T(8,128)}, f32[16,128]{1,0:T(8,128)}, f32[8,128]{1,0:T(8,128)}, f32[256,128]{1,0:T(8,128)}) custom-call(f32[512,128]{1,0:T(8,128)} %get-tuple-element.12.refs_0_, f32[16,128]{1,0:T(8,128)} %get-tuple-element.13.refs_1_, f32[8,128]{1,0:T(8,128)} %get-tuple-element.14.refs_2_, f32[256,128]{1,0:T(8,128)} %get-tuple-element.15.refs_3_), custom_call_target="tpu_custom_call" | custom-call | tf_op jit(solution)/shard_map/hand_over/pallas_call | solution.py:589

commit v4 on v3

--- a/solution.py
+++ b/solution.py
@@ -318,25 +318,24 @@
     each("stage_one", 0)
     for dz in range(1, n["z"]):
         few.stage_one(dz)
-    each("stage_two", 0)
+    each("stage_one", 1)
     for dz in range(n["z"]):
         few.stage_two(dz)
-    each("stage_one", 1)
+    each("stage_two", 0)
+    each("stage_one", 2)
     for dz in range(n["z"]):
         few.stage_core(dz)
-    each("stage_core", 0)
     each("stage_two", 1)
     load.wait()
 
-    def widen(quarter):
-        def step(a, carry):
-            row = pl.multiple_of(a * pitch, 8)
-            wide_ref[pl.ds(row, bi), :] = observed_ref[a].astype(F32)
-            return carry
-
-        lax.fori_loop(bu * quarter // n["z"], bu * (quarter + 1) // n["z"], step, 0, unroll=4)
-
-    widen(0)
+    def widen(a, carry):
+        row = pl.multiple_of(a * pitch, 8)
+        wide_ref[pl.ds(row, bi), :] = observed_ref[a].astype(F32)
+        return carry
+
+    lax.fori_loop(0, bu, widen, 0, unroll=4)
+    each("stage_one", 3)
+    each("stage_two", 2)
     for dz in range(n["z"]):
         for dc in range(1, n["c"]):
             few.end(dz, dc)
@@ -395,17 +394,19 @@
 
         lax.fori_loop(0, n["y"], step, 0)
 
-    for k in range(2, n["z"] + 2):
-        each("stage_one", k)
-        forward(k - 2, 0)
-        each("stage_two", k)
-        each("stage_core", k - 1)
-        if k - 1 <= last:
-            widen(k - 1)
-        for dc in range(1, n["c"]):
-            for flow in flows:
-                flow.end(k - 2, dc)
-            forward(k - 2, dc)
+    for k in range(n["z"] + 1):
+        each("stage_core", k)
+        if k <= last:
+            forward(k, 0)
+        if k + 4 <= last:
+            each("stage_one", k + 4)
+        if k + 3 <= last:
+            each("stage_two", k + 3)
+        if k >= 1:
+            for dc in range(1, n["c"]):
+                for flow in flows:
+                    flow.end(k - 1, dc)
+                forward(k - 1, dc)
 
     wide_b = 8
 
@@ -483,15 +484,15 @@
             carry = backward(dz, dc, carry)
         for flow in sums:
             flow.start(dz)
-        if k >= 1:
-            for flow in sums:
-                flow.stage_two(turns[k - 1])
         carry = backward(dz, 0, carry)
         for flow in sums:
             flow.stage_one(dz)
         if k >= 1:
             for flow in sums:
-                flow.stage_three(turns[k - 1])
+                flow.stage_two(turns[k - 1])
+        if k >= 2:
+            for flow in sums:
+                flow.stage_three(turns[k - 2])
 
     grad_item, grad_ctx = carry
     grad_item, grad_ctx = grad_item * scale, grad_ctx * scale
@@ -509,14 +510,17 @@
     few_sums = ScatterFlow(wires, grid, at, few_terms_ref, few_part, "x", "y", little)
     for dz in turns:
         few_sums.start(dz)
+    if len(turns) >= 2:
+        for flow in sums:
+            flow.stage_three(turns[-2])
+    for dz in turns:
+        few_sums.stage_one(dz)
     for flow in sums:
         flow.stage_two(turns[-1])
     for dz in turns:
-        few_sums.stage_one(dz)
+        few_sums.stage_two(dz)
     for flow in sums:
         flow.stage_three(turns[-1])
-    for dz in turns:
-        few_sums.stage_two(dz)
     for dz in turns:
         few_sums.stage_three(dz)
 

time: 92.1 us -> 84.2 us (0.914)
  Pallas kernels: 89.4 us -> 81.5 us
    pallas_call x1, Pallas kernels: 87.6 us -> 79.7 us  [whole(): pl.pallas_call(functools.partial(whole_kernel, grid, scale), out_shape=tu...]
where the time goes in v4:
time: 84.2 us; the launch traced here: 84.1 us
  Pallas kernels  81.5 us (97%)
  between operations  2.58 us (3%)
    pallas_call x1, Pallas kernels, whole(): pl.pallas_call(functools.partial(whole_kernel, grid, scale), out_shape=tu...  79.7 us
    pallas_call x1, Pallas kernels, hand_over(): pl.pallas_call(hand_over_kernel, out_shape=tuple((jax.ShapeDtypeStruct(a....  1.77 us

profile of v4, /device:TPU:0, one launch (start us, length us, event | category | flops | bytes accessed | tf_op | source)
XLA Modules:
  0.0 84.1 jit_solution(8694080650493819536)
XLA Ops:
  2.6 79.7 %tucker_gradient.1 = (f32[512,128]{1,0:T(8,128)}, f32[16,128]{1,0:T(8,128)}, f32[8,128]{1,0:T(8,128)}, f32[256,128]{1,0:T(8,128)}) custom-call(s32[1]{0:T(128)S(6)} %copy.13.user_block_ref, s32[1]{0:T(128)S(6)} %copy.14.item_block_ref, s32[1]{0:T(128)S(6)} %copy.15.stratum_ref, s32[1,128]{1,0:T(1,128)} %ids_ref.1, bf16[128,128,128]{2,1,0:T(8,128)(2,1)} %bitcast.1, ...), custom_call_target="tpu_custom_call" | custom-call | flops 4831838208 | bytes 4194304 | tf_op jit(solution)/shard_map/tucker_gradient/pallas_call | solution.py:551
  82.3 1.8 %hand_over.1 = (f32[512,128]{1,0:T(8,128)}, f32[16,128]{1,0:T(8,128)}, f32[8,128]{1,0:T(8,128)}, f32[256,128]{1,0:T(8,128)}) custom-call(f32[512,128]{1,0:T(8,128)} %get-tuple-element.12.refs_0_, f32[16,128]{1,0:T(8,128)} %get-tuple-element.13.refs_1_, f32[8,128]{1,0:T(8,128)} %get-tuple-element.14.refs_2_, f32[256,128]{1,0:T(8,128)} %get-tuple-element.15.refs_3_), custom_call_target="tpu_custom_call" | custom-call | tf_op jit(solution)/shard_map/hand_over/pallas_call | solution.py:593

commit v5 on v2

--- a/solution.py
+++ b/solution.py
@@ -367,25 +367,30 @@
         c = lax.rem(at["c"] + dc, n["c"])
         return ((z * n["y"] + y) * n["c"] + c) * n["x"]
 
+    def lanes(value):
+        blocks_here = value.shape[0] // rank_two
+        return jnp.concatenate(
+            [value[j * rank_two:(j + 1) * rank_two] for j in range(blocks_here)], axis=1
+        )
+
+    def cores_at(shards):
+        return jnp.concatenate(
+            [cores_ref[pl.ds(s, n["x"]), :, :].reshape(group, rank) for s in shards], axis=0
+        )
+
     def forward(dz, dc):
-        def step(dy, carry):
-            shard = first_shard(-dz, dy, dc)
-            core = cores_ref[pl.ds(shard, n["x"]), :, :].reshape(group, rank)
-            first = dot(core, ctx_turned, 1, 0).astype(BF16)
+        shards = [first_shard(-dz, dy, dc) for dy in range(n["y"])]
+        first = dot(cores_at(shards), ctx_turned, 1, 0).astype(BF16)
+        second = dot(item_rows, lanes(first), 1, 0)
+        for i, shard in enumerate(shards):
             row = pl.multiple_of(shard * m, group)
-            first_ref[pl.ds(row, group), :] = first
-            wide = jnp.concatenate(
-                [first[j * rank_two:(j + 1) * rank_two] for j in range(across)], axis=1
-            )
-            second = dot(item_rows, wide, 1, 0)
+            first_ref[pl.ds(row, group), :] = first[i * group:(i + 1) * group]
             p = lax.div(shard * m, rank_two)
             for j in range(across):
+                column = (i * across + j) * kc
                 cube_ref[pl.ds(pl.multiple_of((p + j) * pitch, 8), bi), :] = (
-                    second[:, j * kc:(j + 1) * kc]
+                    second[:, column:column + kc]
                 )
-            return carry
-
-        lax.fori_loop(0, n["y"], step, 0)
 
     last = n["z"] - 1
     for k in range(n["z"] + 3):
@@ -405,7 +410,7 @@
                     flow.end(k - 3, dc)
                 forward(k - 3, dc)
 
-    wide_b = 8
+    wide_b = 16 if bi % 16 == 0 else 8
 
     def middle(k, grad_user):
         b = k * wide_b
@@ -445,34 +450,31 @@
     ]
 
     def backward(dz, dc, carry):
-        def step(dy, carry):
-            grad_item, grad_ctx = carry
-            shard = first_shard(dz, dy, dc)
-            p = lax.div(shard * m, rank_two)
-            row = pl.multiple_of(shard * m, group)
-            core = cores_ref[pl.ds(shard, n["x"]), :, :].reshape(group, rank)
-            wide = jnp.concatenate(
-                [
-                    cube_ref[pl.ds(pl.multiple_of((p + j) * pitch, 8), bi), :].astype(BF16)
-                    for j in range(across)
-                ],
-                axis=1,
+        grad_item, grad_ctx = carry
+        shards = [first_shard(dz, dy, dc) for dy in range(n["y"])]
+        starts = [lax.div(shard * m, rank_two) for shard in shards]
+        core = cores_at(shards)
+        wide = jnp.concatenate(
+            [
+                cube_ref[pl.ds(pl.multiple_of((p + j) * pitch, 8), bi), :].astype(BF16)
+                for p in starts
+                for j in range(across)
+            ],
+            axis=1,
+        )
+        first = [first_ref[pl.ds(pl.multiple_of(s * m, group), group), :] for s in shards]
+        folded = dot(item_turned, wide, 1, 0).astype(BF16)
+        folded = jnp.concatenate(
+            [folded[:, j * kc:(j + 1) * kc] for j in range(folded.shape[1] // kc)], axis=0
+        )
+        grad_core = (dot(folded, ctx_rows, 1, 0) * scale).astype(BF16)
+        for i, shard in enumerate(shards):
+            cores_ref[pl.ds(shard, n["x"]), :, :] = (
+                grad_core[i * group:(i + 1) * group].reshape(n["x"], m, rank)
             )
-            first = first_ref[pl.ds(row, group), :]
-            first = jnp.concatenate(
-                [first[j * rank_two:(j + 1) * rank_two] for j in range(across)], axis=1
-            )
-            grad_item = grad_item + dot(wide, first, 1, 1)
-            folded = dot(item_turned, wide, 1, 0).astype(BF16)
-            folded = jnp.concatenate(
-                [folded[:, j * kc:(j + 1) * kc] for j in range(across)], axis=0
-            )
-            grad_ctx = grad_ctx + dot(folded, core, 0, 0)
-            grad_core = (dot(folded, ctx_rows, 1, 0) * scale).astype(BF16)
-            cores_ref[pl.ds(shard, n["x"]), :, :] = grad_core.reshape(n["x"], m, rank)
-            return grad_item, grad_ctx
-
-        return lax.fori_loop(0, n["y"], step, carry)
+        grad_item = grad_item + dot(wide, lanes(jnp.concatenate(first, axis=0)), 1, 1)
+        grad_ctx = grad_ctx + dot(folded, core, 0, 0)
+        return grad_item, grad_ctx
 
     carry = (jnp.zeros((bi, rank_two), F32), jnp.zeros((kc, rank), F32))
     turns = order(n["z"])
@@ -482,9 +484,8 @@
         for flow in sums:
             flow.start(dz)
         carry = backward(dz, 0, carry)
-        if k + 1 < len(turns):
-            for flow in sums:
-                flow.stage_one(dz)
+        for flow in sums:
+            flow.stage_one(dz)
         if k >= 1:
             for flow in sums:
                 flow.stage_two(turns[k - 1])
@@ -508,15 +509,13 @@
     few_sums = ScatterFlow(wires, grid, at, few_terms_ref, few_part, "x", "y", little)
     for dz in turns:
         few_sums.start(dz)
-    for flow in sums:
-        flow.stage_one(turns[-1])
+    if len(turns) >= 2:
+        for flow in sums:
+            flow.stage_three(turns[-2])
     for dz in turns:
         few_sums.stage_one(dz)
     for flow in sums:
         flow.stage_two(turns[-1])
-    if len(turns) >= 2:
-        for flow in sums:
-            flow.stage_three(turns[-2])
     for dz in turns:
         few_sums.stage_two(dz)
     for flow in sums:

time: 82.3 us -> 78.5 us (0.954)
  Pallas kernels: 79.5 us -> 75.7 us
    pallas_call x1, Pallas kernels: 77.8 us -> 73.9 us  [whole(): pl.pallas_call(functools.partial(whole_kernel, grid, scale), out_shape=tu...]
where the time goes in v5:
time: 78.5 us; the launch traced here: 78.3 us
  Pallas kernels  75.7 us (96%)
  between operations  2.58 us (3%)
    pallas_call x1, Pallas kernels, whole(): pl.pallas_call(functools.partial(whole_kernel, grid, scale), out_shape=tu...  73.9 us
    pallas_call x1, Pallas kernels, hand_over(): pl.pallas_call(hand_over_kernel, out_shape=tuple((jax.ShapeDtypeStruct(a....  1.77 us

profile of v5, /device:TPU:0, one launch (start us, length us, event | category | flops | bytes accessed | tf_op | source)
XLA Modules:
  0.0 78.3 jit_solution(12052481828636980745)
XLA Ops:
  2.6 73.9 %tucker_gradient.1 = (f32[512,128]{1,0:T(8,128)}, f32[16,128]{1,0:T(8,128)}, f32[8,128]{1,0:T(8,128)}, f32[256,128]{1,0:T(8,128)}) custom-call(s32[1]{0:T(128)S(6)} %copy.13.user_block_ref, s32[1]{0:T(128)S(6)} %copy.14.item_block_ref, s32[1]{0:T(128)S(6)} %copy.15.stratum_ref, s32[1,128]{1,0:T(1,128)} %ids_ref.1, bf16[128,128,128]{2,1,0:T(8,128)(2,1)} %bitcast.1, ...), custom_call_target="tpu_custom_call" | custom-call | flops 4831838208 | bytes 4194304 | tf_op jit(solution)/shard_map/tucker_gradient/pallas_call | solution.py:550
  76.5 1.8 %hand_over.1 = (f32[512,128]{1,0:T(8,128)}, f32[16,128]{1,0:T(8,128)}, f32[8,128]{1,0:T(8,128)}, f32[256,128]{1,0:T(8,128)}) custom-call(f32[512,128]{1,0:T(8,128)} %get-tuple-element.12.refs_0_, f32[16,128]{1,0:T(8,128)} %get-tuple-element.13.refs_1_, f32[8,128]{1,0:T(8,128)} %get-tuple-element.14.refs_2_, f32[256,128]{1,0:T(8,128)} %get-tuple-element.15.refs_3_), custom_call_target="tpu_custom_call" | custom-call | tf_op jit(solution)/shard_map/hand_over/pallas_call | solution.py:592
